TPU v7x, 32 devices: a whole 2x2x4 slice. The times are simulated.
32 devices in a mesh: groups: 2 (over y), sector: 4 (over z), term: 2 (over x), rep: 2 (over core).
Axes of the slice: x: 2, y: 2, z: 4, core: 2. Of those that a mesh axis runs over, the one named last changes fastest.
Arguments:
- wave_block: bfloat16 [16, 512, 512], P(('groups', 'sector'), 'rep', 'term'), parts along dimension 0
- left_env: bfloat16 [24, 16, 512, 512], P('term', ('groups', 'sector'), 'rep'), parts along dimension 1
- right_env: bfloat16 [24, 16, 512, 512], P('term', ('groups', 'sector')), parts along dimension 1
- term_shift: int32 [24], P('term'), may hold values from -1 to 1
- left_sizes: int32 [16], P(('groups', 'sector')), parts along dimension 0, may hold values from 128 to 512, as said below
- right_sizes: int32 [16], P(('groups', 'sector')), parts along dimension 0, may hold values from 128 to 512, as said below
Outputs:
- next_vector: bfloat16 [16, 512, 512], P(('groups', 'sector'), 'rep', 'term'), parts along dimension 0
- coefficients: float32 [12], P('groups'), parts along dimension 0
There are 2 independent parts, one for each index of `groups`. A program takes and returns all parts, laid end to end along the dimension named above; an argument that names none is the same for every part. Nothing has to cross between parts.
Inputs may be any that keep to these rules, and one draw needn't show every extreme that they name: `left_sizes`: one sector has exactly 512 live left states. `right_sizes`: one sector has exactly 512 live right states.
All inputs are finite; a program needn't handle non-finite values.
Results may differ from a plain program's by a relative error of at most 0.013.
Values may be sent and summed in bfloat16 or wider, within the bound.
A program may use at most 64 MiB of HBM per device.

v0:
```python
import jax
import jax.numpy as jnp
from jax import lax
from jax.sharding import PartitionSpec as P

STEPS = 3


def padded(block, sides, width):
    for axis, dim in sides:
        count = lax.axis_size(axis)
        forward = [(i, i + 1) for i in range(count - 1)]
        backward = [(target, source) for source, target in forward]
        low = lax.ppermute(
            lax.slice_in_dim(block, block.shape[dim] - width, None, axis=dim), axis, forward
        )
        high = lax.ppermute(lax.slice_in_dim(block, 0, width, axis=dim), axis, backward)
        block = jnp.concatenate([low, block, high], axis=dim)
    return block


def total_squares(values):
    return lax.psum(jnp.sum(values * values), ("sector", "term", "rep"))


def on_device(wave_block, left_env, right_env, term_shift, left_sizes, right_sizes):
    block_width = left_env.shape[3]
    row_part = wave_block.shape[1]
    col_part = wave_block.shape[2]
    local_sectors = wave_block.shape[0]
    row_ids = lax.axis_index("rep") * row_part + jnp.arange(row_part, dtype=jnp.int32)
    col_ids = lax.axis_index("term") * col_part + jnp.arange(col_part, dtype=jnp.int32)
    occupied = (row_ids[None, :, None] < left_sizes[:, None, None]) & (
        col_ids[None, None, :] < right_sizes[:, None, None]
    )
    entries = jnp.float32(local_sectors * lax.axis_size("sector") * block_width * block_width)
    shifts = term_shift[:, None, None, None]
    masked_start = jnp.where(occupied, wave_block.astype(jnp.float32), jnp.float32(0.0))
    start_scale = jnp.sqrt(total_squares(masked_start) / entries + 1e-06)
    vector = (masked_start / start_scale).astype(jnp.bfloat16)
    previous = jnp.zeros(vector.shape, jnp.bfloat16)
    beta_now = jnp.float32(0.0)
    alphas = []
    betas = []
    for number in range(STEPS):
        row_whole = lax.all_gather(vector, "rep", axis=1, tiled=True)
        whole = lax.all_gather(row_whole, "term", axis=2, tiled=True)
        extended = padded(whole, (("sector", 0),), 1)
        from_below = extended[:local_sectors]
        from_same = extended[1 : local_sectors + 1]
        from_above = extended[2:]
        source = jnp.where(
            shifts == 1, from_below[None], jnp.where(shifts == 0, from_same[None], from_above[None])
        )
        partial_value = jnp.einsum(
            "wjrk,wjkc->wjrc", left_env, source, preferred_element_type=jnp.float32
        ).astype(jnp.bfloat16)
        summed = jnp.einsum(
            "wjrc,wjce->jre", partial_value, right_env, preferred_element_type=jnp.float32
        )
        summed_share = lax.psum_scatter(summed, "term", scatter_dimension=2, tiled=True)
        image_now = jnp.where(occupied, summed_share, jnp.float32(0.0))
        alpha_now = (
            lax.psum(jnp.sum(vector.astype(jnp.float32) * image_now), ("sector", "term", "rep"))
            / entries
        )
        residual = (
            image_now
            - alpha_now * vector.astype(jnp.float32)
            - beta_now * previous.astype(jnp.float32)
        )
        beta_now = jnp.sqrt(total_squares(residual) / entries + 1e-06)
        previous = vector
        vector = (residual / beta_now).astype(jnp.bfloat16)
        alphas.append(alpha_now)
        betas.append(beta_now)
    return (vector, jnp.stack(alphas + betas))


def solution(mesh):
    in_specs = (
        P(("groups", "sector"), "rep", "term"),
        P("term", ("groups", "sector"), "rep", None),
        P("term", ("groups", "sector"), None, None),
        P("term"),
        P(("groups", "sector")),
        P(("groups", "sector")),
    )
    out_specs = (P(("groups", "sector"), "rep", "term"), P("groups"))
    return jax.shard_map(
        on_device, mesh=mesh, in_specs=in_specs, out_specs=out_specs, check_vma=False
    )
```

profile of v0, /device:TPU:0, one launch (start us, length us, event | category | flops | bytes accessed | tf_op | source)
XLA Modules:
  0.0 488.2 jit_solution(12300139124319183203)
XLA Ops:
  7.2 0.0 all-gather.4.cloned.1.call-start
  7.2 0.7 broadcast_compare_fusion
  8.0 1.8 multiply_reduce_fusion.3
  9.8 35.5 %psum.49 = f32[]{:T(128)} all-reduce(f32[]{:T(128)} %multiply_reduce_fusion.3), channel_id=1, replica_groups=mesh['groups'=2,'sector'=4,'term'=2,'rep'=2] {'sector','term','rep'}, use_global_device_ids=true, to_apply=%region_1.2 | all-reduce | flops 1 | bytes 8 | tf_op jit(solution)/shard_map/psum | solution.py:23
  46.0 1.1 divide_convert_fusion.3
  47.1 2.3 all_gather.18
  49.4 0.0 all-gather.4.cloned.1.call-update
  49.4 0.0 reduce-scatter.4.cloned.1.call-start
  49.5 18.7 %all-gather.4.cloned.1.call-done = bf16[2,512,512]{2,1,0:T(8,128)(2,1)} async-done(((bf16[2,512,256]{2,1,0:T(8,128)(2,1)}), bf16[2,512,512]{2,1,0:T(8,128)(2,1)}) %all-gather.4.cloned.1.call-update) | async-done | bytes 1048592 | tf_op jit(solution)/shard_map/all_gather | solution.py:47
  68.1 1.3 fusion.73
  69.4 3.4 collective-permute-start
  72.8 1.3 collective-permute-start.1
  74.1 0.7 broadcast_compare_fusion.3
  74.8 9.2 %collective-permute-done = bf16[1,512,512]{2,1,0:T(8,128)(2,1)S(1)} collective-permute-done((bf16[1,512,512]{2,1,0:T(8,128)(2,1)S(1)}, bf16[1,512,512]{2,1,0:T(8,128)(2,1)S(1)}, u32[]{:S(2)}, u32[]{:S(2)}) %collective-permute-start) | collective-permute-done | bytes 524320 | tf_op jit(solution)/shard_map/ppermute | solution.py:14
  84.0 4.1 collective-permute-done.1
  88.1 1.4 pad_maximum_fusion.5
  89.5 0.0 copy-start
  89.5 13.0 %fusion.36 = f32[2,256,512]{2,1,0:T(8,128)} fusion(bf16[12,2,512,512]{3,2,1,0:T(8,128)(2,1)} %param.8, bf16[12,2,256,512]{3,2,1,0:T(8,128)(2,1)} %param.7, pred[12]{0:T(512)(128)(4,1)S(1)} %get-tuple-element.15, pred[12]{0:T(512)(128)(4,1)S(1)} %get-tuple-element.14, bf16[2,512,512]{2,1,0:T(8,128)(2,1)S(1)} %get-tuple-element.11, ...), kind=kOutput, calls=%fused_computation.24 | convolution fusion | flops 6458179584 | bytes 23068696 | tf_op jit(solution)/shard_map/wjrc,wjce->jre/dot_general | solution.py:58
  102.5 0.0 reduce-scatter.4.cloned.1.call-update
  102.5 0.0 all-gather.6.cloned.1.call-start
  102.6 19.5 %reduce-scatter.4.cloned.1.call-done = f32[2,256,256]{2,1,0:T(8,128)} async-done(((f32[2,256,512]{2,1,0:T(8,128)}), f32[2,256,256]{2,1,0:T(8,128)}) %reduce-scatter.4.cloned.1.call-update) | async-done | bytes 524304 | tf_op jit(solution)/shard_map/reduce_scatter | solution.py:61
  122.0 1.9 fusion.66
  124.0 32.8 %psum.50 = f32[]{:T(128)} all-reduce(f32[]{:T(128)} %fusion.66), channel_id=1, replica_groups=mesh['groups'=2,'sector'=4,'term'=2,'rep'=2] {'sector','term','rep'}, use_global_device_ids=true, to_apply=%region_4.5 | all-reduce | flops 1 | bytes 8 | tf_op jit(solution)/shard_map/psum | solution.py:64
  157.4 1.9 multiply_reduce_fusion.2
  159.4 30.1 %psum.51 = f32[]{:T(128)} all-reduce(f32[]{:T(128)} %multiply_reduce_fusion.2), channel_id=1, replica_groups=mesh['groups'=2,'sector'=4,'term'=2,'rep'=2] {'sector','term','rep'}, use_global_device_ids=true, to_apply=%region_6.7 | all-reduce | flops 1 | bytes 8 | tf_op jit(solution)/shard_map/psum | solution.py:23
  190.2 1.3 divide_convert_fusion.2
  191.5 2.3 all_gather.20
  193.8 0.0 all-gather.6.cloned.1.call-update
  193.8 0.0 reduce-scatter.6.cloned.1.call-start
  193.8 18.6 %all-gather.6.cloned.1.call-done = bf16[2,512,512]{2,1,0:T(8,128)(2,1)} async-done(((bf16[2,512,256]{2,1,0:T(8,128)(2,1)}), bf16[2,512,512]{2,1,0:T(8,128)(2,1)}) %all-gather.6.cloned.1.call-update) | async-done | bytes 1048592 | tf_op jit(solution)/shard_map/all_gather | solution.py:47
  212.5 1.3 fusion.72
  213.7 3.4 collective-permute-start.2
  217.2 1.3 collective-permute-start.3
  218.5 9.8 %collective-permute-done.2 = bf16[1,512,512]{2,1,0:T(8,128)(2,1)S(1)} collective-permute-done((bf16[1,512,512]{2,1,0:T(8,128)(2,1)S(1)}, bf16[1,512,512]{2,1,0:T(8,128)(2,1)S(1)}, u32[]{:S(2)}, u32[]{:S(2)}) %collective-permute-start.2) | collective-permute-done | bytes 524320 | tf_op jit(solution)/shard_map/ppermute | solution.py:14
  228.3 4.1 collective-permute-done.3
  232.4 1.4 pad_maximum_fusion.3
  233.8 12.9 %fusion.45 = f32[2,256,512]{2,1,0:T(8,128)} fusion(bf16[12,2,512,512]{3,2,1,0:T(8,128)(2,1)} %param.8, bf16[12,2,256,512]{3,2,1,0:T(8,128)(2,1)} %param.7, pred[12]{0:T(512)(128)(4,1)S(1)} %get-tuple-element.15, pred[12]{0:T(512)(128)(4,1)S(1)} %get-tuple-element.14, bf16[2,512,512]{2,1,0:T(8,128)(2,1)S(1)} %get-tuple-element.7, ...), kind=kOutput, calls=%fused_computation.25 | convolution fusion | flops 6458179584 | bytes 23068696 | tf_op jit(solution)/shard_map/wjrc,wjce->jre/dot_general | solution.py:58
  246.8 0.0 reduce-scatter.6.cloned.1.call-update
  246.8 0.0 all-gather.8.cloned.1.call-start
  246.8 19.5 %reduce-scatter.6.cloned.1.call-done = f32[2,256,256]{2,1,0:T(8,128)} async-done(((f32[2,256,512]{2,1,0:T(8,128)}), f32[2,256,256]{2,1,0:T(8,128)}) %reduce-scatter.6.cloned.1.call-update) | async-done | bytes 524304 | tf_op jit(solution)/shard_map/reduce_scatter | solution.py:61
  266.3 1.9 fusion.69
  268.2 32.9 %psum.52 = f32[]{:T(128)} all-reduce(f32[]{:T(128)} %fusion.69), channel_id=1, replica_groups=mesh['groups'=2,'sector'=4,'term'=2,'rep'=2] {'sector','term','rep'}, use_global_device_ids=true, to_apply=%region_9.10 | all-reduce | flops 1 | bytes 8 | tf_op jit(solution)/shard_map/psum | solution.py:64
  301.7 2.0 multiply_reduce_fusion.1
  303.7 30.1 %psum.53 = f32[]{:T(128)} all-reduce(f32[]{:T(128)} %multiply_reduce_fusion.1), channel_id=1, replica_groups=mesh['groups'=2,'sector'=4,'term'=2,'rep'=2] {'sector','term','rep'}, use_global_device_ids=true, to_apply=%region_11.12 | all-reduce | flops 1 | bytes 8 | tf_op jit(solution)/shard_map/psum | solution.py:23
  334.5 1.3 divide_convert_fusion.1
  335.8 2.3 all_gather.22
  338.1 0.0 all-gather.8.cloned.1.call-update
  338.1 0.0 reduce-scatter.8.cloned.1.call-start
  338.2 18.6 %all-gather.8.cloned.1.call-done = bf16[2,512,512]{2,1,0:T(8,128)(2,1)} async-done(((bf16[2,512,256]{2,1,0:T(8,128)(2,1)}), bf16[2,512,512]{2,1,0:T(8,128)(2,1)}) %all-gather.8.cloned.1.call-update) | async-done | bytes 1048592 | tf_op jit(solution)/shard_map/all_gather | solution.py:47
  356.8 1.3 fusion.71
  358.1 3.4 collective-permute-start.4
  361.5 1.5 collective-permute-start.5
  363.0 9.7 %collective-permute-done.4 = bf16[1,512,512]{2,1,0:T(8,128)(2,1)S(1)} collective-permute-done((bf16[1,512,512]{2,1,0:T(8,128)(2,1)S(1)}, bf16[1,512,512]{2,1,0:T(8,128)(2,1)S(1)}, u32[]{:S(2)}, u32[]{:S(2)}) %collective-permute-start.4) | collective-permute-done | bytes 524320 | tf_op jit(solution)/shard_map/ppermute | solution.py:14
  372.6 4.1 collective-permute-done.5
  376.8 1.4 pad_maximum_fusion.1
  378.2 12.9 %fusion.54 = f32[2,256,512]{2,1,0:T(8,128)} fusion(bf16[12,2,512,512]{3,2,1,0:T(8,128)(2,1)} %param.8, bf16[12,2,256,512]{3,2,1,0:T(8,128)(2,1)} %param.7, pred[12]{0:T(512)(128)(4,1)S(1)} %get-tuple-element.15, pred[12]{0:T(512)(128)(4,1)S(1)} %get-tuple-element.14, bf16[2,512,512]{2,1,0:T(8,128)(2,1)S(1)} %get-tuple-element.3, ...), kind=kOutput, calls=%fused_computation.26 | convolution fusion | flops 6458179584 | bytes 23068696 | tf_op jit(solution)/shard_map/wjrc,wjce->jre/dot_general | solution.py:58
  391.1 0.0 reduce-scatter.8.cloned.1.call-update
  391.1 19.5 %reduce-scatter.8.cloned.1.call-done = f32[2,256,256]{2,1,0:T(8,128)} async-done(((f32[2,256,512]{2,1,0:T(8,128)}), f32[2,256,256]{2,1,0:T(8,128)}) %reduce-scatter.8.cloned.1.call-update) | async-done | bytes 524304 | tf_op jit(solution)/shard_map/reduce_scatter | solution.py:61
  410.6 1.9 fusion.63
  412.5 32.9 %psum.54 = f32[]{:T(128)} all-reduce(f32[]{:T(128)} %fusion.63), channel_id=1, replica_groups=mesh['groups'=2,'sector'=4,'term'=2,'rep'=2] {'sector','term','rep'}, use_global_device_ids=true, to_apply=%region_14.15 | all-reduce | flops 1 | bytes 8 | tf_op jit(solution)/shard_map/psum | solution.py:64
  446.0 1.9 multiply_reduce_fusion
  448.0 30.1 %psum.55 = f32[]{:T(128)} all-reduce(f32[]{:T(128)} %multiply_reduce_fusion), channel_id=1, replica_groups=mesh['groups'=2,'sector'=4,'term'=2,'rep'=2] {'sector','term','rep'}, use_global_device_ids=true, to_apply=%region_16.17 | all-reduce | flops 1 | bytes 8 | tf_op jit(solution)/shard_map/psum | solution.py:23
  478.8 0.6 stack.27
  479.4 2.0 divide_convert_fusion
  (3 shorter events, 0.0 us)
Async XLA Ops:
  7.2 61.0 %all-gather.4.cloned.1.call-start = ((), (), s32[]{:S(2)}) async-start(), calls=%async_computation.3 | async-start | bytes 1572864 | tf_op jit(solution)/shard_map/all_gather | solution.py:47
  49.4 72.6 %reduce-scatter.4.cloned.1.call-start = ((), (), s32[]{:S(2)}) async-start(), calls=%async_computation.4 | async-start | bytes 1572864 | tf_op jit(solution)/shard_map/reduce_scatter | solution.py:61
  69.4 14.6 %collective-permute-start = (bf16[1,512,512]{2,1,0:T(8,128)(2,1)S(1)}, bf16[1,512,512]{2,1,0:T(8,128)(2,1)S(1)}, u32[]{:S(2)}, u32[]{:S(2)}) collective-permute-start(bf16[1,512,512]{2,1,0:T(8,128)(2,1)S(1)} %get-tuple-element.12), channel_id=1, source_target_pairs={{0,4},{4,8},{8,12},{1,5},{5,9},{9,13},{2,6},{6,10},{10,14},{3,7},{... | collective-permute-start | bytes 1572872 | tf_op jit(solution)/shard_map/ppermute | solution.py:14
  72.8 15.3 %collective-permute-start.1 = (bf16[1,512,512]{2,1,0:T(8,128)(2,1)S(1)}, bf16[1,512,512]{2,1,0:T(8,128)(2,1)S(1)}, u32[]{:S(2)}, u32[]{:S(2)}) collective-permute-start(bf16[1,512,512]{2,1,0:T(8,128)(2,1)S(1)} %get-tuple-element.13), channel_id=1, source_target_pairs={{4,0},{8,4},{12,8},{5,1},{9,5},{13,9},{6,2},{10,6},{14,10},{7,3},{... | collective-permute-start | bytes 1572872 | tf_op jit(solution)/shard_map/ppermute | solution.py:17
  89.5 32.5 %copy-start = (bf16[2,256,256]{2,1,0:T(8,128)(2,1)S(1)}, bf16[2,256,256]{2,1,0:T(8,128)(2,1)}, u32[]{:S(2)}) copy-start(bf16[2,256,256]{2,1,0:T(8,128)(2,1)} %param.6) | copy-start | bytes 786436
  102.5 109.9 %all-gather.6.cloned.1.call-start = ((), (), s32[]{:S(2)}) async-start(), calls=%async_computation.5 | async-start | bytes 1572864 | tf_op jit(solution)/shard_map/all_gather | solution.py:47
  193.8 72.5 %reduce-scatter.6.cloned.1.call-start = ((), (), s32[]{:S(2)}) async-start(), calls=%async_computation.6 | async-start | bytes 1572864 | tf_op jit(solution)/shard_map/reduce_scatter | solution.py:61
  213.7 14.6 %collective-permute-start.2 = (bf16[1,512,512]{2,1,0:T(8,128)(2,1)S(1)}, bf16[1,512,512]{2,1,0:T(8,128)(2,1)S(1)}, u32[]{:S(2)}, u32[]{:S(2)}) collective-permute-start(bf16[1,512,512]{2,1,0:T(8,128)(2,1)S(1)} %get-tuple-element.8), channel_id=1, source_target_pairs={{0,4},{4,8},{8,12},{1,5},{5,9},{9,13},{2,6},{6,10},{10,14},{3,7},{... | collective-permute-start | bytes 1572872 | tf_op jit(solution)/shard_map/ppermute | solution.py:14
  217.2 15.3 %collective-permute-start.3 = (bf16[1,512,512]{2,1,0:T(8,128)(2,1)S(1)}, bf16[1,512,512]{2,1,0:T(8,128)(2,1)S(1)}, u32[]{:S(2)}, u32[]{:S(2)}) collective-permute-start(bf16[1,512,512]{2,1,0:T(8,128)(2,1)S(1)} %get-tuple-element.9), channel_id=1, source_target_pairs={{4,0},{8,4},{12,8},{5,1},{9,5},{13,9},{6,2},{10,6},{14,10},{7,3},{... | collective-permute-start | bytes 1572872 | tf_op jit(solution)/shard_map/ppermute | solution.py:17
  246.8 110.0 %all-gather.8.cloned.1.call-start = ((), (), s32[]{:S(2)}) async-start(), calls=%async_computation.7 | async-start | bytes 1572864 | tf_op jit(solution)/shard_map/all_gather | solution.py:47
  338.1 72.5 %reduce-scatter.8.cloned.1.call-start = ((), (), s32[]{:S(2)}) async-start(), calls=%async_computation.8 | async-start | bytes 1572864 | tf_op jit(solution)/shard_map/reduce_scatter | solution.py:61
  358.1 14.6 %collective-permute-start.4 = (bf16[1,512,512]{2,1,0:T(8,128)(2,1)S(1)}, bf16[1,512,512]{2,1,0:T(8,128)(2,1)S(1)}, u32[]{:S(2)}, u32[]{:S(2)}) collective-permute-start(bf16[1,512,512]{2,1,0:T(8,128)(2,1)S(1)} %get-tuple-element.4), channel_id=1, source_target_pairs={{0,4},{4,8},{8,12},{1,5},{5,9},{9,13},{2,6},{6,10},{10,14},{3,7},{... | collective-permute-start | bytes 1572872 | tf_op jit(solution)/shard_map/ppermute | solution.py:14
  361.5 15.3 %collective-permute-start.5 = (bf16[1,512,512]{2,1,0:T(8,128)(2,1)S(1)}, bf16[1,512,512]{2,1,0:T(8,128)(2,1)S(1)}, u32[]{:S(2)}, u32[]{:S(2)}) collective-permute-start(bf16[1,512,512]{2,1,0:T(8,128)(2,1)S(1)} %get-tuple-element.5), channel_id=1, source_target_pairs={{4,0},{8,4},{12,8},{5,1},{9,5},{13,9},{6,2},{10,6},{14,10},{7,3},{... | collective-permute-start | bytes 1572872 | tf_op jit(solution)/shard_map/ppermute | solution.py:17
Sparse Core Ops, SparseCore 0:
  49.6 18.5 all-gather.3
  102.6 19.3 reduce-scatter.3
  193.9 18.4 all-gather.5
  246.9 19.3 reduce-scatter.5
  338.2 18.5 all-gather.7
  391.2 19.3 reduce-scatter.7
where the time goes:
time: 489 us; the launch traced here: 488 us
  blocking collectives  231 us (47%)
  waiting for transfers between devices  156 us (32%)
  matrix products  38.8 us (8%)
  other arithmetic  24.5 us (5%)
  between operations  19 us (4%)
  starting transfers between devices  14.6 us (3%)
    psum x4, blocking collectives, total_squares(): return lax.psum(jnp.sum(values * values), ('sector', 'term', 'rep'))  126 us
    psum x3, blocking collectives, on_device(): lax.psum(jnp.sum(vector.astype(jnp.float32) * image_now), ('sector', 'ter...  98.5 us
    reduce_scatter x3, waiting for transfers between devices, on_device(): lax.psum_scatter(summed, 'term', scatter_dimension=2, tiled=True)  58.5 us
    all_gather x3, waiting for transfers between devices, on_device(): whole = lax.all_gather(row_whole, 'term', axis=2, tiled=True)  55.9 us
    dot_general x3, matrix products, on_device(): jnp.einsum('wjrc,wjce->jre', partial_value, right_env, preferred_element_...  38.8 us
    ppermute x3, waiting for transfers between devices, padded(): lax.ppermute(lax.slice_in_dim(block, block.shape[dim] - width, None, axis...  28.7 us
    ppermute x3, waiting for transfers between devices, padded(): lax.ppermute(lax.slice_in_dim(block, 0, width, axis=dim), axis, backward)  12.4 us
    ppermute x3, starting transfers between devices, padded(): lax.ppermute(lax.slice_in_dim(block, block.shape[dim] - width, None, axis...  10.3 us
  transfers between devices with their start and end apart: 12, of which 12 were waited for; matrix products, arithmetic and copies ran while one was open for 0% of the time, Pallas kernels for 0%

commit v1 on v0

v1 whole, which is shorter than its diff:
```python
import functools

import jax
import jax.numpy as jnp
from jax import lax
from jax.experimental import pallas as pl
from jax.experimental.pallas import tpu as pltpu
from jax.sharding import PartitionSpec as P

STEPS = 3
MESH_ID = pl.DeviceIdType.MESH


def largest_divisor(count, limit):
    return max(d for d in range(1, limit + 1) if count % d == 0)


def kernel(
    sectors_n, terms_n, reps_n,
    shift_ref, left_size_ref, right_size_ref, wave_ref, left_hbm, right_hbm,
    out_ref, coef_ref,
    left, right, vec, part, acc, share_out, share_in, red,
    load_sem, x_send, piece_recv, z_send, core_send, core_recv,
    share_send, share_recv, red_send, red_recv,
):
    local_n, rows, cols = wave_ref.shape
    width = left.shape[3]
    terms_local = left.shape[1]
    peers = sectors_n * terms_n * reps_n
    entries = jnp.float32(local_n * sectors_n * width * width)
    z = lax.axis_index("sector")
    x = lax.axis_index("term")
    c = lax.axis_index("rep")
    me = (z * terms_n + x) * reps_n + c
    not_first = z > 0
    not_last = z < sectors_n - 1
    row0 = pl.multiple_of(c * rows, rows)
    other_row0 = pl.multiple_of((1 - c) * rows, rows)

    def place(number):
        return {
            "sector": number // (terms_n * reps_n),
            "term": (number // reps_n) % terms_n,
            "rep": number % reps_n,
        }

    def side(offset):
        return lax.rem(x + offset, terms_n)

    loads = []
    for j in range(local_n):
        loads.append((
            pltpu.make_async_copy(left_hbm.at[:, j], left.at[j], load_sem.at[j, 0]),
            pltpu.make_async_copy(right_hbm.at[:, j], right.at[j], load_sem.at[j, 1]),
        ))
    for pair in loads:
        for copy in pair:
            copy.start()

    barrier = pltpu.get_barrier_semaphore()

    def greet(i, carry):
        pl.semaphore_signal(
            barrier, inc=1, device_id=place(lax.rem(me + i, peers)), device_id_type=MESH_ID
        )
        return carry

    lax.fori_loop(1, peers, greet, 0)

    def fold(values):
        row = jnp.sum(values, axis=0, keepdims=True)
        return sum(row[:, i : i + 128] for i in range(0, row.shape[1], 128))

    def share_sum(slot, row):
        red[slot, me] = row

        def send(i, carry):
            pltpu.make_async_remote_copy(
                src_ref=red.at[slot, me], dst_ref=red.at[slot, me],
                send_sem=red_send.at[slot], recv_sem=red_recv.at[slot],
                device_id=place(lax.rem(me + i, peers)), device_id_type=MESH_ID,
            ).start()
            return carry

        lax.fori_loop(1, peers, send, 0)

    def whole_sum(slot):
        pltpu.make_async_remote_copy(
            src_ref=red.at[slot, pl.ds(0, peers - 1)], dst_ref=red.at[slot, pl.ds(0, peers - 1)],
            send_sem=red_send.at[slot], recv_sem=red_recv.at[slot],
            device_id=place(lax.rem(me + 1, peers)), device_id_type=MESH_ID,
        ).wait()
        return jnp.sum(jnp.sum(red[slot], axis=0), axis=1, keepdims=True) / entries

    def piece(k, s, t):
        return vec.at[k, s, t, pl.ds(row0, rows)]

    def x_copy(k, j, offset, source):
        return pltpu.make_async_remote_copy(
            src_ref=piece(k, 1 + j, source), dst_ref=piece(k, 1 + j, source),
            send_sem=x_send.at[k, j, offset], recv_sem=piece_recv.at[k, 1 + j, source],
            device_id={"term": side(offset)}, device_id_type=MESH_ID,
        )

    def z_copy(k, up, t):
        src = piece(k, local_n if up else 1, t)
        s = 0 if up else local_n + 1
        target = lax.rem(z + (1 if up else sectors_n - 1), sectors_n)
        return pltpu.make_async_remote_copy(
            src_ref=src, dst_ref=piece(k, s, t),
            send_sem=z_send.at[k, int(up), t], recv_sem=piece_recv.at[k, s, t],
            device_id={"sector": target}, device_id_type=MESH_ID,
        )

    def core_copy(k, s, t, start=row0):
        ref = vec.at[k, s, t, pl.ds(start, rows)]
        return pltpu.make_async_remote_copy(
            src_ref=ref, dst_ref=ref,
            send_sem=core_send.at[k, s, t], recv_sem=core_recv.at[k, s, t],
            device_id={"rep": 1 - c}, device_id_type=MESH_ID,
        )

    def send_along_z(k, j, t):
        if sectors_n > 1 and j == 0:
            @pl.when(not_first)
            def _():
                z_copy(k, False, t).start()
        if sectors_n > 1 and j == local_n - 1:
            @pl.when(not_last)
            def _():
                z_copy(k, True, t).start()

    def send_own(k, j):
        for offset in range(1, terms_n):
            x_copy(k, j, offset, x).start()
        send_along_z(k, j, x)
        core_copy(k, 1 + j, x).start()

    edges = ((0, True, not_first), (local_n + 1, False, not_last)) if sectors_n > 1 else ()

    def gather_rest(k):
        for j in range(local_n):
            for offset in range(1, terms_n):
                t = side(offset)
                x_copy(k, j, offset, t).wait_recv()
                send_along_z(k, j, t)
                core_copy(k, 1 + j, t).start()
        for offset in range(terms_n):
            t = side(offset)
            for s, up, there in edges:
                @pl.when(there)
                def _():
                    z_copy(k, up, t).wait_recv()
                    core_copy(k, s, t).start()
        for j in range(local_n):
            for t in range(terms_n):
                core_copy(k, 1 + j, t, other_row0).wait_recv()
        for s, up, there in edges:
            @pl.when(there)
            def _():
                for t in range(terms_n):
                    core_copy(k, s, t, other_row0).wait_recv()

    def drain(k):
        for j in range(local_n):
            for offset in range(1, terms_n):
                x_copy(k, j, offset, x).wait_send()
            for t in range(terms_n):
                core_copy(k, 1 + j, t).wait_send()
        for s, up, there in edges:
            @pl.when(there)
            def _():
                for t in range(terms_n):
                    core_copy(k, s, t).wait_send()
                    z_copy(k, not up, t).wait_send()

    def share_copy(k, j, offset):
        return pltpu.make_async_remote_copy(
            src_ref=share_out.at[j, offset], dst_ref=share_in.at[k, j, terms_n - offset],
            send_sem=share_send.at[k, j, offset], recv_sem=share_recv.at[k, j, terms_n - offset],
            device_id={"term": side(offset)}, device_id_type=MESH_ID,
        )

    def first_products(k, j):
        def body(w, carry):
            s = j + 1 - shift_ref[w]
            for t in range(terms_n):
                at = pl.multiple_of(w * width + t * cols, cols)
                part[j, :, pl.ds(at, cols)] = jnp.dot(
                    left[j, w], vec[k, s, t], preferred_element_type=jnp.float32
                ).astype(jnp.bfloat16)
            return carry

        lax.fori_loop(0, terms_local, body, 0)

    group = largest_divisor(terms_local, 4)

    def second_products(j, offset):
        col0 = pl.multiple_of(side(offset) * cols, cols)
        depth = group * width

        def product(g):
            at = pl.multiple_of(g * depth, depth)
            env = right[j, pl.ds(g * group, group), :, pl.ds(col0, cols)]
            return jnp.dot(
                part[j, :, pl.ds(at, depth)], env.reshape(depth, cols),
                preferred_element_type=jnp.float32,
            )

        acc[j, offset] = jnp.zeros((rows, cols), jnp.float32)

        def body(g, carry):
            acc[j, offset] += product(g)
            return carry

        lax.fori_loop(0, terms_local // group, body, 0)

    def own(k, j):
        return vec[k, 1 + j, x, pl.ds(row0, rows)].astype(jnp.float32)

    row_ids = row0 + lax.broadcasted_iota(jnp.int32, (rows, cols), 0)
    col_ids = x * cols + lax.broadcasted_iota(jnp.int32, (rows, cols), 1)

    def occupied(j):
        return (row_ids < left_size_ref[j]) & (col_ids < right_size_ref[j])

    squares = jnp.zeros((1, 128), jnp.float32)
    for j in range(local_n):
        start = jnp.where(occupied(j), wave_ref[j].astype(jnp.float32), 0.0)
        vec[0, 1 + j, x, pl.ds(row0, rows)] = start.astype(jnp.bfloat16)
        squares += fold(start * start)

    pl.semaphore_wait(barrier, peers - 1)
    for j in range(local_n):
        send_own(0, j)
    share_sum(0, squares)

    def clear(k, s):
        for t in range(terms_n):
            vec[k, s, t] = jnp.zeros((width, cols), jnp.bfloat16)

    @pl.when(jnp.logical_not(not_first))
    def _():
        for k in range(STEPS):
            clear(k, 0)

    @pl.when(jnp.logical_not(not_last))
    def _():
        for k in range(STEPS):
            clear(k, local_n + 1)

    alphas, norms, inverse = [], [], []
    for k in range(STEPS):
        gather_rest(k)
        for j in range(local_n):
            if k == 0:
                loads[j][0].wait()
            first_products(k, j)
            if k == 0:
                loads[j][1].wait()
            for offset in range(1, terms_n):
                second_products(j, offset)
                share_out[j, offset] = acc[j, offset].astype(jnp.bfloat16)
                share_copy(k, j, offset).start()
        for j in range(local_n):
            second_products(j, 0)
        norm = jnp.sqrt(whole_sum(2 * k) + 1e-06)
        scale = 1.0 / norm
        norms.append(norm)
        inverse.append(scale)
        overlap = jnp.zeros((1, 128), jnp.float32)
        for j in range(local_n):
            for offset in range(terms_n):
                held = vec[k, 1 + j, side(offset), pl.ds(row0, rows)].astype(jnp.float32)
                overlap += fold((held * scale) * (acc[j, offset] * scale))
        share_sum(2 * k + 1, overlap)
        drain(k)
        alpha = whole_sum(2 * k + 1)
        alphas.append(alpha)
        squares = jnp.zeros((1, 128), jnp.float32)
        for j in range(local_n):
            image = acc[j, 0]
            for offset in range(1, terms_n):
                share_copy(k, j, terms_n - offset).wait_recv()
                image += share_in[k, j, offset].astype(jnp.float32)
            residual = jnp.where(occupied(j), image * scale, 0.0) - (alpha * scale) * own(k, j)
            if k > 0:
                residual -= (norm * inverse[k - 1]) * own(k - 1, j)
            if k < STEPS - 1:
                vec[k + 1, 1 + j, x, pl.ds(row0, rows)] = residual.astype(jnp.bfloat16)
                send_own(k + 1, j)
            else:
                acc[j, 0] = residual
            squares += fold(residual * residual)
        share_sum(2 * k + 2, squares)
        for j in range(local_n):
            for offset in range(1, terms_n):
                share_copy(k, j, offset).wait_send()
    norm = jnp.sqrt(whole_sum(2 * STEPS) + 1e-06)
    norms.append(norm)
    scale = 1.0 / norm
    for j in range(local_n):
        out_ref[j] = (acc[j, 0] * scale).astype(jnp.bfloat16)
    lanes = lax.broadcasted_iota(jnp.int32, (1, 128), 1)
    row = jnp.zeros((1, 128), jnp.float32)
    for i, value in enumerate(alphas + norms[1:]):
        row = jnp.where(lanes == i, value, row)
    coef_ref[...] = row[:, : 2 * STEPS]


def on_device(sizes, wave_block, left_env, right_env, term_shift, left_sizes, right_sizes):
    local_n, rows, cols = wave_block.shape
    terms_local, _, _, width = left_env.shape
    sectors_n, terms_n, reps_n = sizes
    peers = sectors_n * terms_n * reps_n
    slots = local_n + 2
    dma = pltpu.SemaphoreType.DMA
    smem = pl.BlockSpec(memory_space=pltpu.SMEM)
    vmem = pl.BlockSpec(memory_space=pltpu.VMEM)
    hbm = pl.BlockSpec(memory_space=pl.ANY)
    bf16, f32 = jnp.bfloat16, jnp.float32
    vector, coefficients = pl.pallas_call(
        functools.partial(kernel, sectors_n, terms_n, reps_n),
        out_shape=(
            jax.ShapeDtypeStruct((local_n, rows, cols), bf16),
            jax.ShapeDtypeStruct((1, 2 * STEPS), f32),
        ),
        in_specs=[smem, smem, smem, vmem, hbm, hbm],
        out_specs=(vmem, vmem),
        scratch_shapes=[
            pltpu.VMEM((local_n, terms_local, rows, width), bf16),
            pltpu.VMEM((local_n, terms_local, width, width), bf16),
            pltpu.VMEM((STEPS, slots, terms_n, width, cols), bf16),
            pltpu.VMEM((local_n, rows, terms_local * width), bf16),
            pltpu.VMEM((local_n, terms_n, rows, cols), f32),
            pltpu.VMEM((local_n, terms_n, rows, cols), bf16),
            pltpu.VMEM((STEPS, local_n, terms_n, rows, cols), bf16),
            pltpu.VMEM((2 * STEPS + 1, peers, 1, 128), f32),
            dma((local_n, 2)),
            dma((STEPS, local_n, terms_n)),
            dma((STEPS, slots, terms_n)),
            dma((STEPS, 2, terms_n)),
            dma((STEPS, slots, terms_n)),
            dma((STEPS, slots, terms_n)),
            dma((STEPS, local_n, terms_n)),
            dma((STEPS, local_n, terms_n)),
            dma((2 * STEPS + 1,)),
            dma((2 * STEPS + 1,)),
        ],
        compiler_params=pltpu.CompilerParams(
            collective_id=0, has_side_effects=True, vmem_limit_bytes=56 * 1024 * 1024
        ),
    )(term_shift, left_sizes, right_sizes, wave_block, left_env, right_env)
    return vector, coefficients.reshape(2 * STEPS)


def solution(mesh):
    in_specs = (
        P(("groups", "sector"), "rep", "term"),
        P("term", ("groups", "sector"), "rep", None),
        P("term", ("groups", "sector"), None, None),
        P("term"),
        P(("groups", "sector")),
        P(("groups", "sector")),
    )
    out_specs = (P(("groups", "sector"), "rep", "term"), P("groups"))
    sizes = (mesh.shape["sector"], mesh.shape["term"], mesh.shape["rep"])
    return jax.shard_map(
        functools.partial(on_device, sizes), mesh=mesh, in_specs=in_specs, out_specs=out_specs,
        check_vma=False,
    )
```

time: 489 us -> 105 us (0.21)
  blocking collectives: 231 us -> 0 us
  waiting for transfers between devices: 156 us -> 0 us
  Pallas kernels: 0 us -> 102 us
  matrix products: 38.8 us -> 0 us
  other arithmetic: 24.5 us -> 0 us
  between operations: 19 us -> 0.64 us
  starting transfers between devices: 14.6 us -> 0 us
    psum x7 -> x0, blocking collectives: 224 us -> none  [the longest x4 126 us: total_squares(): return lax.psum(jnp.sum(values * values), ('sector', 'term', 'rep'))]
    pallas_call x0 -> x1, Pallas kernels: none -> 102 us  [on_device(): pl.pallas_call(functools.partial(kernel, sectors_n, terms_n, reps_n), out...]
    reduce_scatter x3 -> x0, waiting for transfers between devices: 58.5 us -> none  [on_device(): lax.psum_scatter(summed, 'term', scatter_dimension=2, tiled=True)]
    all_gather x3 -> x0, waiting for transfers between devices: 55.9 us -> none  [on_device(): whole = lax.all_gather(row_whole, 'term', axis=2, tiled=True)]
    ppermute x6 -> x0, waiting for transfers between devices: 41.1 us -> none  [the longest x3 28.7 us: padded(): lax.ppermute(lax.slice_in_dim(block, block.shape[dim] - width, None, axis...]
    dot_general x3 -> x0, matrix products: 38.8 us -> none  [on_device(): jnp.einsum('wjrc,wjce->jre', partial_value, right_env, preferred_element_...]
    ppermute x6 -> x0, starting transfers between devices: 14.3 us -> none  [the longest x3 10.3 us: padded(): lax.ppermute(lax.slice_in_dim(block, block.shape[dim] - width, None, axis...]
    reduce_sum x7 -> x0, other arithmetic: 13.3 us -> none  [the longest x4 7.64 us: total_squares(): return lax.psum(jnp.sum(values * values), ('sector', 'term', 'rep'))]
  transfers between devices with their start and end apart: 12 -> 0, of which waited for: 12 -> 0; matrix products, arithmetic and copies ran while one was open for 0% -> 0% of each run, Pallas kernels for 0% -> 0%
where the time goes in v1:
time: 105 us
  Pallas kernels  102 us (97%)
  local copies, waits for them, and re-layouts  2.8 us (3%)
    pallas_call x1, Pallas kernels, on_device(): pl.pallas_call(functools.partial(kernel, sectors_n, terms_n, reps_n), out...  102 us
    unnamed x2, local copies, waits for them, and re-layouts  2.8 us

profile of v1, /device:TPU:0, one launch (start us, length us, event | category | flops | bytes accessed | tf_op | source)
XLA Modules:
  0.0 105.1 jit_solution(2895254381936496629)
XLA Ops:
  0.6 101.6 %shard_map.77 = (bf16[2,256,256]{2,1,0:T(8,128)(2,1)}, f32[1,6]{1,0:T(1,128)}) custom-call(s32[12]{0:T(128)} %shift_ref.1, s32[2]{0:T(128)} %left_size_ref.1, s32[2]{0:T(128)} %right_size_ref.1, bf16[2,256,256]{2,1,0:T(8,128)(2,1)} %wave_ref.1, bf16[12,2,256,512]{3,2,1,0:T(8,128)(2,1)} %left_hbm.1, bf16[12,2,512,512]{3,2,1,0:T(8,128)(2,1)} %right_hbm.1), custom_call_target="tpu_custom_call" | custom-call | tf_op jit(solution)/shard_map/pallas_call | solution.py:322
  102.3 1.7 %copy.10 = bf16[2,256,256]{2,1,0:T(8,128)(2,1)} copy(bf16[2,256,256]{2,1,0:T(8,128)(2,1)} %get-tuple-element.8) | data formatting | bytes 524288
  103.9 1.1 %copy.11 = f32[6]{0:T(128)} copy(f32[6]{0:T(128)} %bitcast.1) | data formatting | bytes 48

commit v2 on v1

--- a/solution.py
+++ b/solution.py
@@ -8,6 +8,8 @@
 from jax.sharding import PartitionSpec as P
 
 STEPS = 3
+CHUNKS = 2
+UNROLL = 2
 MESH_ID = pl.DeviceIdType.MESH
 
 
@@ -19,7 +21,7 @@
     sectors_n, terms_n, reps_n,
     shift_ref, left_size_ref, right_size_ref, wave_ref, left_hbm, right_hbm,
     out_ref, coef_ref,
-    left, right, vec, part, acc, share_out, share_in, red,
+    left, right, near, far, part, acc, share_out, share_in, red,
     load_sem, x_send, piece_recv, z_send, core_send, core_recv,
     share_send, share_recv, red_send, red_recv,
 ):
@@ -35,7 +37,7 @@
     not_first = z > 0
     not_last = z < sectors_n - 1
     row0 = pl.multiple_of(c * rows, rows)
-    other_row0 = pl.multiple_of((1 - c) * rows, rows)
+    height = rows // CHUNKS
 
     def place(number):
         return {
@@ -92,87 +94,92 @@
         ).wait()
         return jnp.sum(jnp.sum(red[slot], axis=0), axis=1, keepdims=True) / entries
 
-    def piece(k, s, t):
-        return vec.at[k, s, t, pl.ds(row0, rows)]
-
-    def x_copy(k, j, offset, source):
+    def chunk(k, s, offset, q, core):
+        at = pl.ds(pl.multiple_of(core * rows + q * height, height), height)
+        return near.at[k, s, at] if offset == 0 else far.at[k, s, offset - 1, at]
+
+    def x_copy(k, j, offset, q):
         return pltpu.make_async_remote_copy(
-            src_ref=piece(k, 1 + j, source), dst_ref=piece(k, 1 + j, source),
-            send_sem=x_send.at[k, j, offset], recv_sem=piece_recv.at[k, 1 + j, source],
+            src_ref=chunk(k, 1 + j, 0, q, c), dst_ref=chunk(k, 1 + j, terms_n - offset, q, c),
+            send_sem=x_send.at[k, j, offset, q],
+            recv_sem=piece_recv.at[k, 1 + j, terms_n - offset, q],
             device_id={"term": side(offset)}, device_id_type=MESH_ID,
         )
 
-    def z_copy(k, up, t):
-        src = piece(k, local_n if up else 1, t)
+    def z_copy(k, up, offset, q):
         s = 0 if up else local_n + 1
         target = lax.rem(z + (1 if up else sectors_n - 1), sectors_n)
         return pltpu.make_async_remote_copy(
-            src_ref=src, dst_ref=piece(k, s, t),
-            send_sem=z_send.at[k, int(up), t], recv_sem=piece_recv.at[k, s, t],
+            src_ref=chunk(k, local_n if up else 1, offset, q, c),
+            dst_ref=chunk(k, s, offset, q, c),
+            send_sem=z_send.at[k, int(up), offset, q], recv_sem=piece_recv.at[k, s, offset, q],
             device_id={"sector": target}, device_id_type=MESH_ID,
         )
 
-    def core_copy(k, s, t, start=row0):
-        ref = vec.at[k, s, t, pl.ds(start, rows)]
+    def core_copy(k, s, offset, q, core=c):
+        ref = chunk(k, s, offset, q, core)
         return pltpu.make_async_remote_copy(
             src_ref=ref, dst_ref=ref,
-            send_sem=core_send.at[k, s, t], recv_sem=core_recv.at[k, s, t],
+            send_sem=core_send.at[k, s, offset, q], recv_sem=core_recv.at[k, s, offset, q],
             device_id={"rep": 1 - c}, device_id_type=MESH_ID,
         )
 
-    def send_along_z(k, j, t):
+    def send_along_z(k, j, offset, q):
         if sectors_n > 1 and j == 0:
             @pl.when(not_first)
             def _():
-                z_copy(k, False, t).start()
+                z_copy(k, False, offset, q).start()
         if sectors_n > 1 and j == local_n - 1:
             @pl.when(not_last)
             def _():
-                z_copy(k, True, t).start()
+                z_copy(k, True, offset, q).start()
 
     def send_own(k, j):
-        for offset in range(1, terms_n):
-            x_copy(k, j, offset, x).start()
-        send_along_z(k, j, x)
-        core_copy(k, 1 + j, x).start()
+        for q in range(CHUNKS):
+            for offset in range(1, terms_n):
+                x_copy(k, j, offset, q).start()
+            send_along_z(k, j, 0, q)
+            core_copy(k, 1 + j, 0, q).start()
+
+    def pass_on(k, j):
+        for q in range(CHUNKS):
+            for offset in range(1, terms_n):
+                x_copy(k, j, terms_n - offset, q).wait_recv()
+                send_along_z(k, j, offset, q)
+                core_copy(k, 1 + j, offset, q).start()
 
     edges = ((0, True, not_first), (local_n + 1, False, not_last)) if sectors_n > 1 else ()
 
-    def gather_rest(k):
-        for j in range(local_n):
-            for offset in range(1, terms_n):
-                t = side(offset)
-                x_copy(k, j, offset, t).wait_recv()
-                send_along_z(k, j, t)
-                core_copy(k, 1 + j, t).start()
-        for offset in range(terms_n):
-            t = side(offset)
+    def pass_edges(k, offset):
+        for q in range(CHUNKS):
             for s, up, there in edges:
                 @pl.when(there)
                 def _():
-                    z_copy(k, up, t).wait_recv()
-                    core_copy(k, s, t).start()
-        for j in range(local_n):
-            for t in range(terms_n):
-                core_copy(k, 1 + j, t, other_row0).wait_recv()
-        for s, up, there in edges:
-            @pl.when(there)
-            def _():
-                for t in range(terms_n):
-                    core_copy(k, s, t, other_row0).wait_recv()
+                    z_copy(k, up, offset, q).wait_recv()
+                    core_copy(k, s, offset, q).start()
+
+    def arrive(k, offset):
+        for q in range(CHUNKS):
+            for j in range(local_n):
+                core_copy(k, 1 + j, offset, q, 1 - c).wait_recv()
+            for s, up, there in edges:
+                @pl.when(there)
+                def _():
+                    core_copy(k, s, offset, q, 1 - c).wait_recv()
 
     def drain(k):
-        for j in range(local_n):
-            for offset in range(1, terms_n):
-                x_copy(k, j, offset, x).wait_send()
-            for t in range(terms_n):
-                core_copy(k, 1 + j, t).wait_send()
-        for s, up, there in edges:
-            @pl.when(there)
-            def _():
-                for t in range(terms_n):
-                    core_copy(k, s, t).wait_send()
-                    z_copy(k, not up, t).wait_send()
+        for q in range(CHUNKS):
+            for j in range(local_n):
+                for offset in range(1, terms_n):
+                    x_copy(k, j, offset, q).wait_send()
+                for offset in range(terms_n):
+                    core_copy(k, 1 + j, offset, q).wait_send()
+            for s, up, there in edges:
+                @pl.when(there)
+                def _():
+                    for offset in range(terms_n):
+                        core_copy(k, s, offset, q).wait_send()
+                        z_copy(k, not up, offset, q).wait_send()
 
     def share_copy(k, j, offset):
         return pltpu.make_async_remote_copy(
@@ -181,17 +188,19 @@
             device_id={"term": side(offset)}, device_id_type=MESH_ID,
         )
 
-    def first_products(k, j):
+    def first_products(k, j, offset):
+        col0 = side(offset) * cols
+
         def body(w, carry):
             s = j + 1 - shift_ref[w]
-            for t in range(terms_n):
-                at = pl.multiple_of(w * width + t * cols, cols)
-                part[j, :, pl.ds(at, cols)] = jnp.dot(
-                    left[j, w], vec[k, s, t], preferred_element_type=jnp.float32
-                ).astype(jnp.bfloat16)
+            source = near[k, s] if offset == 0 else far[k, s, offset - 1]
+            at = pl.multiple_of(w * width + col0, cols)
+            part[j, :, pl.ds(at, cols)] = jnp.dot(
+                left[j, w], source, preferred_element_type=jnp.float32
+            ).astype(jnp.bfloat16)
             return carry
 
-        lax.fori_loop(0, terms_local, body, 0)
+        lax.fori_loop(0, terms_local, body, 0, unroll=largest_divisor(terms_local, UNROLL))
 
     group = largest_divisor(terms_local, 4)
 
@@ -216,7 +225,7 @@
         lax.fori_loop(0, terms_local // group, body, 0)
 
     def own(k, j):
-        return vec[k, 1 + j, x, pl.ds(row0, rows)].astype(jnp.float32)
+        return near[k, 1 + j, pl.ds(row0, rows)].astype(jnp.float32)
 
     row_ids = row0 + lax.broadcasted_iota(jnp.int32, (rows, cols), 0)
     col_ids = x * cols + lax.broadcasted_iota(jnp.int32, (rows, cols), 1)
@@ -227,7 +236,7 @@
     squares = jnp.zeros((1, 128), jnp.float32)
     for j in range(local_n):
         start = jnp.where(occupied(j), wave_ref[j].astype(jnp.float32), 0.0)
-        vec[0, 1 + j, x, pl.ds(row0, rows)] = start.astype(jnp.bfloat16)
+        near[0, 1 + j, pl.ds(row0, rows)] = start.astype(jnp.bfloat16)
         squares += fold(start * start)
 
     pl.semaphore_wait(barrier, peers - 1)
@@ -236,8 +245,8 @@
     share_sum(0, squares)
 
     def clear(k, s):
-        for t in range(terms_n):
-            vec[k, s, t] = jnp.zeros((width, cols), jnp.bfloat16)
+        near[k, s] = jnp.zeros((width, cols), jnp.bfloat16)
+        far[k, s] = jnp.zeros(far.shape[2:], jnp.bfloat16)
 
     @pl.when(jnp.logical_not(not_first))
     def _():
@@ -251,11 +260,22 @@
 
     alphas, norms, inverse = [], [], []
     for k in range(STEPS):
-        gather_rest(k)
+        pass_on(k, 0)
+        pass_edges(k, 0)
+        arrive(k, 0)
         for j in range(local_n):
             if k == 0:
                 loads[j][0].wait()
-            first_products(k, j)
+            first_products(k, j, 0)
+            if j < local_n - 1:
+                pass_on(k, j + 1)
+        for offset in range(1, terms_n):
+            pass_edges(k, offset)
+        for offset in range(1, terms_n):
+            arrive(k, offset)
+        for j in range(local_n):
+            for offset in range(1, terms_n):
+                first_products(k, j, offset)
             if k == 0:
                 loads[j][1].wait()
             for offset in range(1, terms_n):
@@ -271,7 +291,9 @@
         overlap = jnp.zeros((1, 128), jnp.float32)
         for j in range(local_n):
             for offset in range(terms_n):
-                held = vec[k, 1 + j, side(offset), pl.ds(row0, rows)].astype(jnp.float32)
+                mine = pl.ds(row0, rows)
+                held = near[k, 1 + j, mine] if offset == 0 else far[k, 1 + j, offset - 1, mine]
+                held = held.astype(jnp.float32)
                 overlap += fold((held * scale) * (acc[j, offset] * scale))
         share_sum(2 * k + 1, overlap)
         drain(k)
@@ -287,7 +309,7 @@
             if k > 0:
                 residual -= (norm * inverse[k - 1]) * own(k - 1, j)
             if k < STEPS - 1:
-                vec[k + 1, 1 + j, x, pl.ds(row0, rows)] = residual.astype(jnp.bfloat16)
+                near[k + 1, 1 + j, pl.ds(row0, rows)] = residual.astype(jnp.bfloat16)
                 send_own(k + 1, j)
             else:
                 acc[j, 0] = residual
@@ -330,18 +352,19 @@
         scratch_shapes=[
             pltpu.VMEM((local_n, terms_local, rows, width), bf16),
             pltpu.VMEM((local_n, terms_local, width, width), bf16),
-            pltpu.VMEM((STEPS, slots, terms_n, width, cols), bf16),
+            pltpu.VMEM((STEPS, slots, width, cols), bf16),
+            pltpu.VMEM((STEPS, slots, terms_n - 1, width, cols), bf16),
             pltpu.VMEM((local_n, rows, terms_local * width), bf16),
             pltpu.VMEM((local_n, terms_n, rows, cols), f32),
             pltpu.VMEM((local_n, terms_n, rows, cols), bf16),
             pltpu.VMEM((STEPS, local_n, terms_n, rows, cols), bf16),
             pltpu.VMEM((2 * STEPS + 1, peers, 1, 128), f32),
             dma((local_n, 2)),
-            dma((STEPS, local_n, terms_n)),
-            dma((STEPS, slots, terms_n)),
-            dma((STEPS, 2, terms_n)),
-            dma((STEPS, slots, terms_n)),
-            dma((STEPS, slots, terms_n)),
+            dma((STEPS, local_n, terms_n, CHUNKS)),
+            dma((STEPS, slots, terms_n, CHUNKS)),
+            dma((STEPS, 2, terms_n, CHUNKS)),
+            dma((STEPS, slots, terms_n, CHUNKS)),
+            dma((STEPS, slots, terms_n, CHUNKS)),
             dma((STEPS, local_n, terms_n)),
             dma((STEPS, local_n, terms_n)),
             dma((2 * STEPS + 1,)),

time: 105 us -> 97.9 us (0.932)
  Pallas kernels: 102 us -> 94.3 us
    pallas_call x1, Pallas kernels: 102 us -> 94.3 us  [on_device(): pl.pallas_call(functools.partial(kernel, sectors_n, terms_n, reps_n), out...]
where the time goes in v2:
time: 97.9 us; the launch traced here: 97.8 us
  Pallas kernels  94.3 us (96%)
  local copies, waits for them, and re-layouts  2.8 us (3%)
    pallas_call x1, Pallas kernels, on_device(): pl.pallas_call(functools.partial(kernel, sectors_n, terms_n, reps_n), out...  94.3 us
    unnamed x2, local copies, waits for them, and re-layouts  2.8 us

profile of v2, /device:TPU:0, one launch (start us, length us, event | category | flops | bytes accessed | tf_op | source)
XLA Modules:
  0.0 97.8 jit_solution(11637507486453122702)
XLA Ops:
  0.6 94.3 %shard_map.77 = (bf16[2,256,256]{2,1,0:T(8,128)(2,1)}, f32[1,6]{1,0:T(1,128)}) custom-call(s32[12]{0:T(128)} %shift_ref.1, s32[2]{0:T(128)} %left_size_ref.1, s32[2]{0:T(128)} %right_size_ref.1, bf16[2,256,256]{2,1,0:T(8,128)(2,1)} %wave_ref.1, bf16[12,2,256,512]{3,2,1,0:T(8,128)(2,1)} %left_hbm.1, bf16[12,2,512,512]{3,2,1,0:T(8,128)(2,1)} %right_hbm.1), custom_call_target="tpu_custom_call" | custom-call | tf_op jit(solution)/shard_map/pallas_call | solution.py:344
  95.0 1.7 %copy.10 = bf16[2,256,256]{2,1,0:T(8,128)(2,1)} copy(bf16[2,256,256]{2,1,0:T(8,128)(2,1)} %get-tuple-element.8) | data formatting | bytes 524288
  96.6 1.1 %copy.11 = f32[6]{0:T(128)} copy(f32[6]{0:T(128)} %bitcast.1) | data formatting | bytes 48
